TPU v7x, 1024 devices: a whole 4x8x16 slice. The times are simulated.
1024 devices in a mesh: row: 16 (over z), col: 32 (over y, x), depth: 2 (over core).
Axes of the slice: x: 4, y: 8, z: 16, core: 2. Of those that a mesh axis runs over, the one named last changes fastest.
Arguments:
- density: bfloat16 [1024, 27, 64, 64], P(('row', 'col', 'depth')), may hold values from -1.296875 to 1.296875
- pattern: int32 [1024, 27], P(('row', 'col', 'depth')), may hold values 0 or 1
Outputs:
- square: bfloat16 [1024, 27, 64, 64], P(('row', 'col', 'depth'))
All inputs are finite; a program needn't handle non-finite values. No bound on the sum of `pattern` on one device may be relied on, other than what follows from the above.
Results may differ from a plain program's by a relative error of at most 0.001.
Values may be sent and summed in bfloat16 or wider, within the bound.
A program may use at most 64 MiB of HBM per device.

v0:
```python
import jax
import jax.numpy as jnp
import numpy as np
from jax import lax
from jax.sharding import PartitionSpec as P


def shifted(block, axis, distance):
    devices = range(lax.axis_size(axis))
    route = [((i - distance) % len(devices), i) for i in devices]
    return lax.ppermute(block, axis, route)


def offset_of(slot_id):
    return (slot_id // 9 - 1, slot_id // 3 % 3 - 1, slot_id % 3 - 1)


def block_index(layers, a_near, b_near, z_place, a_rest, b_rest, z_rest):
    if b_near == -1:
        column_place = b_rest
    elif b_near == 0:
        column_place = 3 + b_rest
    else:
        column_place = 6 + b_rest
    first_part = 63 * layers
    if a_near == 0:
        return ((z_place * 3 + a_rest + 1) * 7 + column_place) * 3 + z_rest + 1
    if a_near == -1:
        return first_part + ((z_place * 2 + a_rest) * 7 + column_place) * 3 + z_rest + 1
    return (
        first_part + 42 * layers + ((z_place * 2 + a_rest + 1) * 7 + column_place) * 3 + z_rest + 1
    )


def pair_table(out_rows, layers, z_offset, slot_count):
    lookup = np.full((out_rows, slot_count, 27), 147 * layers, np.int32)
    for out_index in range(out_rows):
        for slot_id in range(27):
            a_step, b_step, z_step = offset_of(slot_id)
            z_place = out_index + z_offset + z_step
            if z_place < 0 or z_place >= layers:
                continue
            for target in range(27):
                a_goal, b_goal, z_goal = offset_of(target)
                a_rest, b_rest, z_rest = (a_goal - a_step, b_goal - b_step, z_goal - z_step)
                if max(abs(a_rest), abs(b_rest), abs(z_rest)) > 1:
                    continue
                lookup[out_index, slot_id, target] = block_index(
                    layers, a_step, b_step, z_place, a_rest, b_rest, z_rest
                )
    return lookup


def shift_along_col(piece, offset_step):
    return shifted(piece, "col", offset_step)


def shift_along_row(piece, offset_step):
    return shifted(piece, "row", offset_step)


def neighbourhood(column):
    layer_total = column.shape[0]
    block_size = column.shape[-1]
    slot_cube = column.reshape(layer_total, 3, 3, 3, block_size, block_size)
    below_col = shift_along_col(slot_cube[:, :, 1:3], 1)
    above_col = shift_along_col(slot_cube[:, :, 0:2], -1)
    merged_col = jnp.concatenate([below_col, slot_cube, above_col], axis=2)
    below_row = shift_along_row(merged_col[:, 1:3], 1)
    above_row = shift_along_row(merged_col[:, 0:2], -1)
    sections = [
        merged_col.reshape(-1, block_size, block_size),
        below_row.reshape(-1, block_size, block_size),
        above_row.reshape(-1, block_size, block_size),
        jnp.zeros((1, block_size, block_size), column.dtype),
    ]
    return jnp.concatenate(sections, axis=0)


def local(density, pattern):
    dev_rows = density.shape[0]
    block_size = density.shape[-1]
    depth_count = lax.axis_size("depth")
    layer_index = lax.axis_index("depth")
    layers = dev_rows * depth_count
    layer_rows = layer_index * dev_rows + jnp.arange(dev_rows, dtype=jnp.int32)
    layer_step = jnp.arange(27, dtype=jnp.int32) % 3 - 1
    layer_near = layer_rows[:, None] + layer_step[None, :]
    inside = (layer_near >= 0) & (layer_near < layers)
    present = jnp.where(inside, pattern, 0)
    weight = present.astype(jnp.bfloat16)
    blocks = density * weight[:, :, None, None]
    slot_share = -(-27 // depth_count)
    slot_count = slot_share * depth_count
    padded = jnp.concatenate(
        [blocks, jnp.zeros((dev_rows, slot_count - 27, block_size, block_size), blocks.dtype)],
        axis=1,
    )
    own_slots = lax.all_to_all(padded, "depth", split_axis=1, concat_axis=0, tiled=True)
    column = lax.all_gather(blocks, "depth", axis=0, tiled=True)
    stacked = neighbourhood(column)
    lookup = jnp.asarray(pair_table(layers, layers, 0, slot_count))
    first_slot = layer_index * slot_share
    chosen = lax.dynamic_slice(
        lookup, (0, first_slot, 0), (dev_rows * lax.axis_size("depth"), slot_share, 27)
    )
    partners = stacked[chosen]
    summed = lax.psum_scatter(
        jnp.einsum("rtab,rtsbc->rsac", own_slots, partners, preferred_element_type=jnp.float32),
        "depth",
        scatter_dimension=0,
        tiled=True,
    )
    return (summed * weight[:, :, None, None]).astype(jnp.bfloat16)


def solution(mesh):
    placed = (P(("row", "col", "depth"), None, None, None), P(("row", "col", "depth"), None))
    return jax.shard_map(
        local,
        mesh=mesh,
        in_specs=placed,
        out_specs=P(("row", "col", "depth"), None, None, None),
        check_vma=False,
    )
```

profile of v0, /device:TPU:1, one launch (start us, length us, event | category | flops | bytes accessed | tf_op | source)
XLA Modules:
  0.0 156.4 jit_solution(5698236033010025556)
XLA Ops:
  6.5 0.7 fusion.2
  7.2 1.1 broadcast_multiply_fusion
  8.3 16.2 %all_gather.3 = bf16[2,27,64,64]{3,2,1,0:T(8,128)(2,1)S(1)} all-gather(bf16[1,27,64,64]{3,2,1,0:T(8,128)(2,1)S(1)} %broadcast_multiply_fusion), channel_id=1, replica_groups=mesh['row'=16,'col'=32,'depth'=2] {'depth'}, dimensions={0}, use_global_device_ids=true | all-gather | bytes 663552 | tf_op jit(solution)/shard_map/all_gather | solution.py:100
  24.5 0.2 fusion.4
  24.8 1.9 %collective-permute-start = (bf16[2,3,2,3,64,64]{5,4,3,2,1,0:T(8,128)(2,1)S(1)}, bf16[2,3,2,3,64,64]{5,4,3,2,1,0:T(8,128)(2,1)S(1)}, u32[]{:S(2)}, u32[]{:S(2)}) collective-permute-start(bf16[2,3,2,3,64,64]{5,4,3,2,1,0:T(8,128)(2,1)S(1)} %get-tuple-element.9), channel_id=1, source_target_pairs={{62,0},{0,2},{2,4},{4,6},{6,8},{8,10},{10,12},{12,14},{14,16},{16,... | collective-permute-start | bytes 884744 | tf_op jit(solution)/shard_map/ppermute | solution.py:11
  26.7 6.7 %collective-permute-start.1 = (bf16[2,3,2,3,64,64]{5,4,3,2,1,0:T(8,128)(2,1)S(1)}, bf16[2,3,2,3,64,64]{5,4,3,2,1,0:T(8,128)(2,1)S(1)}, u32[]{:S(2)}, u32[]{:S(2)}) collective-permute-start(bf16[2,3,2,3,64,64]{5,4,3,2,1,0:T(8,128)(2,1)S(1)} %get-tuple-element.10), channel_id=1, source_target_pairs={{2,0},{4,2},{6,4},{8,6},{10,8},{12,10},{14,12},{16,14},{18,16},{20... | collective-permute-start | bytes 884744 | tf_op jit(solution)/shard_map/ppermute | solution.py:11
  33.4 11.1 %collective-permute-done = bf16[2,3,2,3,64,64]{5,4,3,2,1,0:T(8,128)(2,1)S(1)} collective-permute-done((bf16[2,3,2,3,64,64]{5,4,3,2,1,0:T(8,128)(2,1)S(1)}, bf16[2,3,2,3,64,64]{5,4,3,2,1,0:T(8,128)(2,1)S(1)}, u32[]{:S(2)}, u32[]{:S(2)}) %collective-permute-start) | collective-permute-done | bytes 294944 | tf_op jit(solution)/shard_map/ppermute | solution.py:11
  44.5 0.9 collective-permute-done.1
  45.4 0.5 pad_maximum_fusion
  45.8 2.4 %fusion.3 = (bf16[2,2,7,3,64,64]{5,4,3,2,1,0:T(8,128)(2,1)}, bf16[2,2,7,3,64,64]{5,4,3,2,1,0:T(8,128)(2,1)}) fusion(bf16[2,3,7,3,64,64]{5,4,3,2,1,0:T(8,128)(2,1)S(1)} %pad_maximum_fusion), kind=kLoop, calls=%fused_computation.15 | loop fusion | bytes 2752512 | tf_op jit(solution)/shard_map/slice | solution.py:69
  48.2 0.0 copy-start
  48.2 2.0 %collective-permute-start.2 = (bf16[2,2,7,3,64,64]{5,4,3,2,1,0:T(8,128)(2,1)}, bf16[2,2,7,3,64,64]{5,4,3,2,1,0:T(8,128)(2,1)}, u32[]{:S(2)}, u32[]{:S(2)}) collective-permute-start(bf16[2,2,7,3,64,64]{5,4,3,2,1,0:T(8,128)(2,1)} %get-tuple-element.7), channel_id=1, source_target_pairs={{960,0},{0,64},{64,128},{128,192},{192,256},{256,320},{320,384},{3... | collective-permute-start | bytes 2064392 | tf_op jit(solution)/shard_map/ppermute | solution.py:11
  50.3 6.2 %collective-permute-start.3 = (bf16[2,2,7,3,64,64]{5,4,3,2,1,0:T(8,128)(2,1)}, bf16[2,2,7,3,64,64]{5,4,3,2,1,0:T(8,128)(2,1)}, u32[]{:S(2)}, u32[]{:S(2)}) collective-permute-start(bf16[2,2,7,3,64,64]{5,4,3,2,1,0:T(8,128)(2,1)} %get-tuple-element.8), channel_id=1, source_target_pairs={{64,0},{128,64},{192,128},{256,192},{320,256},{384,320},{448,384},... | collective-permute-start | bytes 2064392 | tf_op jit(solution)/shard_map/ppermute | solution.py:11
  56.5 0.1 fusion.5
  56.6 1.0 reshape.88
  57.7 4.9 %all-to-all-start = ((bf16[2,2,28672]{2,1,0:T(2,128)(2,1)}), bf16[2,2,28672]{2,1,0:T(2,128)(2,1)S(1)}, u32[]{:S(2)}, u32[]{:S(2)}) async-start(bf16[2,2,28672]{2,1,0:T(2,128)(2,1)} %reshape.88), calls=%async_computation | async-start | bytes 458752 | tf_op jit(solution)/shard_map/all_to_all | solution.py:99
  62.6 0.0 reduce-scatter.2.cloned.1.call-start
  62.6 0.0 copy-done
  62.6 0.1 reshape.77
  62.7 0.1 pad.4.clone
  62.8 1.0 all-to-all-done
  63.7 0.3 reshape.89
  64.1 20.1 %collective-permute-done.2 = bf16[2,2,7,3,64,64]{5,4,3,2,1,0:T(8,128)(2,1)} collective-permute-done((bf16[2,2,7,3,64,64]{5,4,3,2,1,0:T(8,128)(2,1)}, bf16[2,2,7,3,64,64]{5,4,3,2,1,0:T(8,128)(2,1)}, u32[]{:S(2)}, u32[]{:S(2)}) %collective-permute-start.2) | collective-permute-done | bytes 688160 | tf_op jit(solution)/shard_map/ppermute | solution.py:11
  84.2 0.9 collective-permute-done.3
  85.1 6.5 %maximum_maximum_fusion = bf16[295,64,64]{2,1,0:T(8,128)(2,1)} fusion(bf16[84,64,64]{2,1,0:T(8,128)(2,1)} %bitcast.4, bf16[84,64,64]{2,1,0:T(8,128)(2,1)} %bitcast.3, bf16[126,64,64]{2,1,0:T(8,128)(2,1)S(1)} %bitcast.33, bf16[295]{0:T(512)(128)(2,1)S(1)} %pad.4.clone), kind=kLoop, calls=%fused_computation.1 | loop fusion | flops 3624960 | bytes 4825678 | tf_op jit(solution)/shard_map/concatenate | solution.py:77
  91.5 21.8 %gather_fusion = bf16[756,64,64]{2,1,0:T(8,128)(2,1)} fusion(bf16[295,64,64]{2,1,0:T(8,128)(2,1)} %maximum_maximum_fusion, s32[1024]{0:T(1024)S(1)} %pad_clamp_fusion), kind=kCustom, calls=%fused_computation | custom fusion | bytes 12389328 | tf_op jit(solution)/shard_map/gather | solution.py:107
  113.3 10.7 %convolution_bitcast_fusion = f32[2,27,64,64]{2,3,1,0:T(8,128)} fusion(bf16[2,14,27,64,64]{4,3,2,1,0:T(8,128)(2,1)} %bitcast.32, bf16[2,14,64,64,1]{3,2,4,1,0:T(8,128)(2,1)S(1)} %bitcast.36), kind=kOutput, calls=%fused_computation.3 | convolution fusion | flops 396361728 | bytes 7307264 | tf_op jit(solution)/shard_map/rtab,rtsbc->rsac/dot_general | solution.py:109
  124.0 0.0 reduce-scatter.2.cloned.1.call-update
  124.0 23.3 %reduce-scatter.2.cloned.1.call-done = f32[1,27,64,64]{2,3,1,0:T(8,128)} async-done(((f32[2,27,64,64]{2,3,1,0:T(8,128)}), f32[1,27,64,64]{2,3,1,0:T(8,128)}) %reduce-scatter.2.cloned.1.call-update) | async-done | bytes 442384 | tf_op jit(solution)/shard_map/reduce_scatter | solution.py:108
  147.3 1.3 multiply_convert_fusion
  148.6 1.0 copy.9
  (2 shorter events, 0.0 us)
Async XLA Ops:
  24.8 19.8 %collective-permute-start = (bf16[2,3,2,3,64,64]{5,4,3,2,1,0:T(8,128)(2,1)S(1)}, bf16[2,3,2,3,64,64]{5,4,3,2,1,0:T(8,128)(2,1)S(1)}, u32[]{:S(2)}, u32[]{:S(2)}) collective-permute-start(bf16[2,3,2,3,64,64]{5,4,3,2,1,0:T(8,128)(2,1)S(1)} %get-tuple-element.9), channel_id=1, source_target_pairs={{62,0},{0,2},{2,4},{4,6},{6,8},{8,10},{10,12},{12,14},{14,16},{16,... | collective-permute-start | bytes 884744 | tf_op jit(solution)/shard_map/ppermute | solution.py:11
  26.7 18.7 %collective-permute-start.1 = (bf16[2,3,2,3,64,64]{5,4,3,2,1,0:T(8,128)(2,1)S(1)}, bf16[2,3,2,3,64,64]{5,4,3,2,1,0:T(8,128)(2,1)S(1)}, u32[]{:S(2)}, u32[]{:S(2)}) collective-permute-start(bf16[2,3,2,3,64,64]{5,4,3,2,1,0:T(8,128)(2,1)S(1)} %get-tuple-element.10), channel_id=1, source_target_pairs={{2,0},{4,2},{6,4},{8,6},{10,8},{12,10},{14,12},{16,14},{18,16},{20... | collective-permute-start | bytes 884744 | tf_op jit(solution)/shard_map/ppermute | solution.py:11
  48.2 14.4 %copy-start = (s32[2,28,27]{2,1,0:T(8,128)S(1)}, s32[2,28,27]{2,1,0:T(8,128)}, u32[]{:S(2)}) copy-start(s32[2,28,27]{2,1,0:T(8,128)} %constant.35.clone) | copy-start | bytes 18148
  48.2 36.0 %collective-permute-start.2 = (bf16[2,2,7,3,64,64]{5,4,3,2,1,0:T(8,128)(2,1)}, bf16[2,2,7,3,64,64]{5,4,3,2,1,0:T(8,128)(2,1)}, u32[]{:S(2)}, u32[]{:S(2)}) collective-permute-start(bf16[2,2,7,3,64,64]{5,4,3,2,1,0:T(8,128)(2,1)} %get-tuple-element.7), channel_id=1, source_target_pairs={{960,0},{0,64},{64,128},{128,192},{192,256},{256,320},{320,384},{3... | collective-permute-start | bytes 2064392 | tf_op jit(solution)/shard_map/ppermute | solution.py:11
  50.3 34.8 %collective-permute-start.3 = (bf16[2,2,7,3,64,64]{5,4,3,2,1,0:T(8,128)(2,1)}, bf16[2,2,7,3,64,64]{5,4,3,2,1,0:T(8,128)(2,1)}, u32[]{:S(2)}, u32[]{:S(2)}) collective-permute-start(bf16[2,2,7,3,64,64]{5,4,3,2,1,0:T(8,128)(2,1)} %get-tuple-element.8), channel_id=1, source_target_pairs={{64,0},{128,64},{192,128},{256,192},{320,256},{384,320},{448,384},... | collective-permute-start | bytes 2064392 | tf_op jit(solution)/shard_map/ppermute | solution.py:11
  57.7 6.1 %all-to-all-start = ((bf16[2,2,28672]{2,1,0:T(2,128)(2,1)}), bf16[2,2,28672]{2,1,0:T(2,128)(2,1)S(1)}, u32[]{:S(2)}, u32[]{:S(2)}) async-start(bf16[2,2,28672]{2,1,0:T(2,128)(2,1)} %reshape.88), calls=%async_computation | async-start | bytes 458752 | tf_op jit(solution)/shard_map/all_to_all | solution.py:99
  62.6 84.7 %reduce-scatter.2.cloned.1.call-start = ((), (), s32[]{:S(2)}) async-start(), calls=%async_computation.2 | async-start | bytes 2654208 | tf_op jit(solution)/shard_map/reduce_scatter | solution.py:108
Sparse Core Ops, SparseCore 0:
  124.1 23.1 reduce-scatter.1
where the time goes:
time: 157 us; the launch traced here: 156 us
  waiting for transfers between devices  57.3 us (36%)
  local copies, waits for them, and re-layouts  27 us (17%)
  starting transfers between devices  21.8 us (14%)
  blocking collectives  16.2 us (10%)
  between operations  13.5 us (9%)
  matrix products  10.7 us (7%)
  other arithmetic  10 us (6%)
    ppermute x4, waiting for transfers between devices, shifted(): return lax.ppermute(block, axis, route)  33 us
    reduce_scatter x1, waiting for transfers between devices, local(): lax.psum_scatter(jnp.einsum('rtab,rtsbc->rsac', own_slots, partners, pref...  23.3 us
    gather x1, local copies, waits for them, and re-layouts, local(): partners = stacked[chosen]  21.8 us
    ppermute x4, starting transfers between devices, shifted(): return lax.ppermute(block, axis, route)  16.9 us
    all_gather x1, blocking collectives, local(): column = lax.all_gather(blocks, 'depth', axis=0, tiled=True)  16.2 us
    dot_general x1, matrix products, local(): jnp.einsum('rtab,rtsbc->rsac', own_slots, partners, preferred_element_typ...  10.7 us
    concatenate x1, other arithmetic, neighbourhood(): return jnp.concatenate(sections, axis=0)  6.46 us
    all_to_all x1, starting transfers between devices, local(): lax.all_to_all(padded, 'depth', split_axis=1, concat_axis=0, tiled=True)  4.91 us
  transfers between devices with their start and end apart: 6, of which 6 were waited for; matrix products, arithmetic and copies ran while one was open for 1% of the time, Pallas kernels for 0%

commit v1 on v0

v1 whole, which is shorter than its diff:
```python
import functools

import jax
import jax.numpy as jnp
from jax import lax
from jax.experimental import pallas as pl
from jax.experimental.pallas import tpu as pltpu
from jax.sharding import PartitionSpec as P

MESH = pl.DeviceIdType.MESH
STEPS = [(a, b) for a in (-1, 0, 1) for b in (-1, 0, 1)]
CENTRE = 4
AWAY = [0, 2, 6, 8, 1, 7, 3, 5]


def pairs_of(t):
    a, b = STEPS[t]
    found = []
    for target, (goal_a, goal_b) in enumerate(STEPS):
        rest = (goal_a - a, goal_b - b)
        if rest in STEPS:
            found.append((target, STEPS.index(rest)))
    return found


def tiles_of(t):
    return -(-len(pairs_of(t)) // 2)


def kernel(
    density_hbm,
    pattern_ref,
    out_ref,
    density,
    kept,
    left,
    outgoing,
    incoming,
    total,
    ship,
    landed,
    load_sem,
    left_sems,
    send_sems,
    recv_sems,
    ship_sems,
):
    rows, cols = lax.axis_size("row"), lax.axis_size("col")
    a, b, z = lax.axis_index("row"), lax.axis_index("col"), lax.axis_index("depth")
    other = 1 - z
    size = density.shape[-1]

    load = pltpu.make_async_copy(density_hbm.at[0], density, load_sem)
    load.start()

    def device(t, layer):
        step_a, step_b = STEPS[t]
        return {
            "row": lax.rem(a - step_a + rows, rows),
            "col": lax.rem(b - step_b + cols, cols),
            "depth": layer,
        }

    barrier = pltpu.get_barrier_semaphore()
    for t in AWAY:
        for layer in range(2):
            pl.semaphore_signal(
                barrier, inc=1, device_id=device(t, layer), device_id_type=MESH
            )
    pl.semaphore_signal(
        barrier, inc=1, device_id=device(CENTRE, other), device_id_type=MESH
    )
    load.wait()

    for slot in range(9):
        for layer in range(2):
            place = 3 * slot + 1 + layer - z
            block = density[place]
            kept[layer, slot] = jnp.where(
                pattern_ref[0, place] != 0, block, jnp.zeros_like(block)
            )
    for slot in range(9):
        left[z, slot] = jnp.concatenate([kept[0, slot], kept[1, slot]], axis=1)
    for t in AWAY + [CENTRE]:
        slots = [slot for _, slot in pairs_of(t)]
        for layer in range(2):
            for j in range(tiles_of(t)):
                first = kept[layer, slots[2 * j]]
                if 2 * j + 1 < len(slots):
                    second = kept[layer, slots[2 * j + 1]]
                else:
                    second = jnp.zeros_like(first)
                outgoing[t, layer, j] = jnp.concatenate([first, second], axis=1)
    for j in range(tiles_of(CENTRE)):
        incoming[CENTRE, z, j] = outgoing[CENTRE, z, j]

    pl.semaphore_wait(barrier, 17)

    copies = []

    def send(src, dst, send_sem, recv_sem, target):
        copy = pltpu.make_async_remote_copy(
            src_ref=src,
            dst_ref=dst,
            send_sem=send_sem,
            recv_sem=recv_sem,
            device_id=target,
            device_id_type=MESH,
        )
        copy.start()
        copies.append(copy)
        return copy

    for t in AWAY:
        count = tiles_of(t)
        for layer in range(2):
            send(
                outgoing.at[t, layer, pl.ds(0, count)],
                incoming.at[t, z, pl.ds(0, count)],
                send_sems.at[t, layer],
                recv_sems.at[t, z],
                device(t, layer),
            )
    sibling = device(CENTRE, other)
    send(left.at[z], left.at[z], left_sems.at[0], left_sems.at[1], sibling)
    send(
        outgoing.at[CENTRE, other],
        incoming.at[CENTRE, z],
        send_sems.at[CENTRE, 0],
        recv_sems.at[CENTRE, z],
        sibling,
    )

    def arrived(ref, sem):
        pltpu.make_async_copy(ref, ref, sem).wait()

    def multiply(t, first):
        count = tiles_of(t)
        lhs = jnp.concatenate([left[0, t], left[1, t]], axis=0)
        tiles = [
            jnp.concatenate([incoming[t, 0, j], incoming[t, 1, j]], axis=0)
            for j in range(count)
        ]
        product = jnp.dot(
            lhs, jnp.concatenate(tiles, axis=1), preferred_element_type=jnp.float32
        )
        for place, (target, _) in enumerate(pairs_of(t)):
            part = product[:, place * size : (place + 1) * size]
            for layer in range(2):
                rows_of = part[layer * size : (layer + 1) * size]
                if first:
                    total[target, layer] = rows_of
                else:
                    total[target, layer] += rows_of

    arrived(left.at[other], left_sems.at[1])
    arrived(incoming.at[CENTRE, other], recv_sems.at[CENTRE, other])
    multiply(CENTRE, True)
    for t in AWAY:
        for layer in range(2):
            arrived(incoming.at[t, layer, pl.ds(0, tiles_of(t))], recv_sems.at[t, layer])
        multiply(t, False)

    for j in range(5):
        first = total[2 * j, other]
        second = total[2 * j + 1, other] if j < 4 else jnp.zeros_like(first)
        ship[j] = jnp.concatenate([first, second], axis=1).astype(ship.dtype)
    send(ship, landed, ship_sems.at[0], ship_sems.at[1], sibling)

    nothing = jnp.zeros((size, size), out_ref.dtype)
    for target in range(9):
        out_ref[0, 3 * target + 1 + z - other] = nothing
        place = 3 * target + 1
        out_ref[0, place] = jnp.where(
            pattern_ref[0, place] != 0, total[target, z].astype(out_ref.dtype), nothing
        )
    arrived(landed, ship_sems.at[1])
    for target in range(9):
        j, half = target // 2, target % 2
        block = landed[j][:, half * size : (half + 1) * size]
        place = 3 * target + 1 + other - z
        out_ref[0, place] = jnp.where(pattern_ref[0, place] != 0, block, nothing)
    for copy in copies:
        copy.wait_send()


def local(density, pattern):
    size = density.shape[-1]
    kind = density.dtype
    wide = 2 * size
    return pl.pallas_call(
        kernel,
        out_shape=jax.ShapeDtypeStruct(density.shape, kind),
        in_specs=[
            pl.BlockSpec(memory_space=pl.ANY),
            pl.BlockSpec(memory_space=pltpu.SMEM),
        ],
        out_specs=pl.BlockSpec(memory_space=pltpu.VMEM),
        scratch_shapes=[
            pltpu.VMEM((27, size, size), kind),
            pltpu.VMEM((2, 9, size, size), kind),
            pltpu.VMEM((2, 9, size, wide), kind),
            pltpu.VMEM((9, 2, 5, size, wide), kind),
            pltpu.VMEM((9, 2, 5, size, wide), kind),
            pltpu.VMEM((9, 2, size, size), jnp.float32),
            pltpu.VMEM((5, size, wide), kind),
            pltpu.VMEM((5, size, wide), kind),
            pltpu.SemaphoreType.DMA,
            pltpu.SemaphoreType.DMA((2,)),
            pltpu.SemaphoreType.DMA((9, 2)),
            pltpu.SemaphoreType.DMA((9, 2)),
            pltpu.SemaphoreType.DMA((2,)),
        ],
        compiler_params=pltpu.CompilerParams(
            collective_id=0,
            has_side_effects=True,
            vmem_limit_bytes=32 * 1024 * 1024,
        ),
    )(density, pattern)


def solution(mesh):
    placed = (P(("row", "col", "depth"), None, None, None), P(("row", "col", "depth"), None))
    return jax.shard_map(
        local,
        mesh=mesh,
        in_specs=placed,
        out_specs=P(("row", "col", "depth"), None, None, None),
        check_vma=False,
    )
```

time: 157 us -> 35.4 us (0.23)
  waiting for transfers between devices: 57.3 us -> 0 us
  Pallas kernels: 0 us -> 32.8 us
  local copies, waits for them, and re-layouts: 27 us -> 2.43 us
  starting transfers between devices: 21.8 us -> 0 us
  blocking collectives: 16.2 us -> 0 us
  between operations: 13.5 us -> 0.01 us
  matrix products: 10.7 us -> 0 us
  other arithmetic: 10 us -> 0 us
    ppermute x4 -> x0, waiting for transfers between devices: 33 us -> none  [shifted(): return lax.ppermute(block, axis, route)]
    pallas_call x0 -> x1, Pallas kernels: none -> 32.8 us  [local(): pl.pallas_call(kernel, out_shape=jax.ShapeDtypeStruct(density.shape, kind...]
    reduce_scatter x1 -> x0, waiting for transfers between devices: 23.3 us -> none  [local(): lax.psum_scatter(jnp.einsum('rtab,rtsbc->rsac', own_slots, partners, pref...]
    gather x1 -> x0, local copies, waits for them, and re-layouts: 21.8 us -> none  [local(): partners = stacked[chosen]]
    ppermute x4 -> x0, starting transfers between devices: 16.9 us -> none  [shifted(): return lax.ppermute(block, axis, route)]
    all_gather x1 -> x0, blocking collectives: 16.2 us -> none  [local(): column = lax.all_gather(blocks, 'depth', axis=0, tiled=True)]
    dot_general x1 -> x0, matrix products: 10.7 us -> none  [local(): jnp.einsum('rtab,rtsbc->rsac', own_slots, partners, preferred_element_typ...]
    concatenate x2 -> x0, other arithmetic: 6.91 us -> none  [the longest x1 6.46 us: neighbourhood(): return jnp.concatenate(sections, axis=0)]
  transfers between devices with their start and end apart: 6 -> 0, of which waited for: 6 -> 0; matrix products, arithmetic and copies ran while one was open for 1% -> 0% of each run, Pallas kernels for 0% -> 0%
where the time goes in v1:
time: 35.4 us; the launch traced here: 35.2 us
  Pallas kernels  32.8 us (93%)
  local copies, waits for them, and re-layouts  2.43 us (7%)
    pallas_call x1, Pallas kernels, local(): pl.pallas_call(kernel, out_shape=jax.ShapeDtypeStruct(density.shape, kind...  32.8 us
    unnamed x5, local copies, waits for them, and re-layouts  2.43 us

profile of v1, /device:TPU:1, one launch (start us, length us, event | category | flops | bytes accessed | tf_op | source)
XLA Modules:
  0.0 35.2 jit_solution(12525904522210880807)
XLA Ops:
  0.0 0.0 copy-start
  0.0 1.0 %copy-done = bf16[1,27,64,64]{3,2,1,0:T(8,128)(2,1)S(1)} copy-done((bf16[1,27,64,64]{3,2,1,0:T(8,128)(2,1)S(1)}, bf16[1,27,64,64]{3,2,1,0:T(8,128)(2,1)}, u32[]{:S(2)}) %copy-start) | copy-done | bytes 221208
  1.0 0.0 copy-start.1
  1.0 0.7 %copy-done.1 = s32[1,27]{1,0:T(1,128)S(1)} copy-done((s32[1,27]{1,0:T(1,128)S(1)}, s32[1,27]{1,0:T(1,128)}, u32[]{:S(2)}) %copy-start.1) | copy-done | bytes 132
  1.7 32.8 %shard_map.28 = bf16[1,27,64,64]{3,2,1,0:T(8,128)(2,1)S(1)} custom-call(bf16[1,27,64,64]{3,2,1,0:T(8,128)(2,1)S(1)} %copy-done, s32[1,27]{1,0:T(1,128)S(1)} %copy-done.1), custom_call_target="tpu_custom_call" | custom-call | tf_op jit(solution)/shard_map/pallas_call | solution.py:191
  34.5 0.8 %copy.4 = bf16[1,27,64,64]{3,2,1,0:T(8,128)(2,1)} copy(bf16[1,27,64,64]{3,2,1,0:T(8,128)(2,1)S(1)} %shard_map.28) | data formatting | bytes 442368
Async XLA Ops:
  0.0 1.0 %copy-start = (bf16[1,27,64,64]{3,2,1,0:T(8,128)(2,1)S(1)}, bf16[1,27,64,64]{3,2,1,0:T(8,128)(2,1)}, u32[]{:S(2)}) copy-start(bf16[1,27,64,64]{3,2,1,0:T(8,128)(2,1)} %density_hbm.1) | copy-start | bytes 663556
  1.0 0.7 %copy-start.1 = (s32[1,27]{1,0:T(1,128)S(1)}, s32[1,27]{1,0:T(1,128)}, u32[]{:S(2)}) copy-start(s32[1,27]{1,0:T(1,128)} %pattern_ref.1) | copy-start | bytes 328

commit v2 on v1

v2 whole, which is shorter than its diff:
```python
import jax
import jax.numpy as jnp
from jax import lax
from jax.experimental import pallas as pl
from jax.experimental.pallas import tpu as pltpu
from jax.sharding import PartitionSpec as P

MESH = pl.DeviceIdType.MESH
STEPS = [(a, b) for a in (-1, 0, 1) for b in (-1, 0, 1)]
CENTRE = 4
ROW_UP = [0, 2, 1]
COLUMN = [3, 5]
ROW_DOWN = [6, 7, 8]
AWAY = ROW_UP + COLUMN + ROW_DOWN

TILES = [
    ((1, -1), (1, 0)),
    ((-1, -1), (0, -1)),
    ((-1, 0), (0, 0)),
    ((-1, 1), (0, 1)),
    ((1, 0), (1, 1)),
    ((0, -1), (1, -1)),
    ((0, 0), (1, 0)),
    ((0, 1), (1, 1)),
]


def tiles_of(t):
    a, b = STEPS[t]
    if a == 0:
        return {-1: (2, 3), 0: (0, 5), 1: (0, 3)}[b]
    first = 5 if a == -1 else 1
    return {-1: (first + 1, 2), 0: (first, 3), 1: (first, 2)}[b]


def kernel(
    density_hbm,
    pattern_hbm,
    out_ref,
    density,
    pattern,
    kept,
    left,
    packed,
    incoming,
    total_low,
    total_high,
    ship,
    landed,
    load_sems,
    credits,
    left_sems,
    send_sems,
    recv_sems,
    ship_sems,
):
    rows, cols = lax.axis_size("row"), lax.axis_size("col")
    a, b, z = lax.axis_index("row"), lax.axis_index("col"), lax.axis_index("depth")
    other = 1 - z
    size = density.shape[-1]

    loads = [
        pltpu.make_async_copy(density_hbm.at[0], density, load_sems.at[0]),
        pltpu.make_async_copy(pattern_hbm, pattern, load_sems.at[1]),
    ]
    for load in loads:
        load.start()

    def place_of(t, layer):
        step_a, step_b = STEPS[t]
        return (
            lax.rem(a - step_a + rows, rows),
            lax.rem(b - step_b + cols, cols),
            layer,
        )

    def device(t, layer):
        return dict(zip(("row", "col", "depth"), place_of(t, layer)))

    def rank(place):
        index = (place[0] * cols + place[1]) * 2 + place[2]
        return jnp.where(index == 0, 8 * cols - 1, 2 * index)

    mine = rank((a, b, z))
    partners = [(t, layer) for t in AWAY for layer in range(2)] + [(CENTRE, other)]
    later = {}
    for t, layer in partners:
        later[t, 0 if t == CENTRE else layer] = rank(place_of(t, layer)) > mine

    def is_later(t, layer):
        return later[t, 0 if t == CENTRE else layer]

    def credit(t, layer):
        return credits.at[t, 0 if t == CENTRE else layer]

    barrier = pltpu.get_barrier_semaphore()
    earlier = jnp.int32(0)
    for t, layer in partners:
        earlier += jnp.where(is_later(t, layer), 0, 1)

        @pl.when(is_later(t, layer))
        def _(t=t, layer=layer):
            pl.semaphore_signal(
                barrier, inc=1, device_id=device(t, layer), device_id_type=MESH
            )

    @pl.when(earlier > 0)
    def _():
        pl.semaphore_wait(barrier, earlier)

    for t, layer in partners:

        @pl.when(jnp.logical_not(is_later(t, layer)))
        def _(t=t, layer=layer):
            pl.semaphore_signal(
                credits.at[8 - t, 0 if t == CENTRE else z],
                inc=1,
                device_id=device(t, layer),
                device_id_type=MESH,
            )

    def ready(t, layer):
        @pl.when(is_later(t, layer))
        def _():
            pl.semaphore_wait(credit(t, layer), 1)

    copies = []

    def copy_to(src, dst, send_sem, recv_sem, target):
        copy = pltpu.make_async_remote_copy(
            src_ref=src,
            dst_ref=dst,
            send_sem=send_sem,
            recv_sem=recv_sem,
            device_id=target,
            device_id_type=MESH,
        )
        copies.append(copy)
        return copy

    def send(t, layer):
        first, count = tiles_of(t)
        return copy_to(
            packed.at[layer, pl.ds(first, count)],
            incoming.at[t, z, pl.ds(0, count)],
            send_sems.at[t, 0 if t == CENTRE else layer],
            recv_sems.at[t, z],
            device(t, layer),
        )

    def keep(slots):
        for slot in slots:
            for layer in range(2):
                place = 3 * slot + 1 + layer - z
                block = density[place]
                kept[layer, slot] = jnp.where(
                    pattern[0, place] != 0, block, jnp.zeros_like(block)
                )

    def pack(tiles):
        for tile in tiles:
            for layer in range(2):
                packed[layer, tile] = jnp.concatenate(
                    [kept[layer, STEPS.index(step)] for step in TILES[tile]], axis=1
                )

    for load in loads:
        load.wait()
    keep(range(3, 9))
    pack(range(5, 8))

    up = [(t, layer, send(t, layer)) for t in ROW_UP for layer in range(2)]
    last_row = a == rows - 1

    def send_up():
        for t, layer, copy in up:
            ready(t, layer)
            copy.start()

    def sent_up():
        for _, _, copy in up:
            copy.wait_send()

    pl.when(last_row)(send_up)
    keep(range(3))
    pack(range(5))
    for slot in range(9):
        left[z, slot] = jnp.concatenate([kept[0, slot], kept[1, slot]], axis=1)
    pl.when(last_row)(sent_up)

    for layer in (1, 0):
        for t in COLUMN:
            ready(t, layer)
            send(t, layer).start()
    sibling = device(CENTRE, other)
    ready(CENTRE, other)
    copy_to(left.at[z], left.at[z], left_sems.at[0], left_sems.at[1], sibling).start()
    send(CENTRE, other).start()
    pl.when(jnp.logical_not(last_row))(send_up)

    down = [(t, layer, send(t, layer)) for layer in (1, 0) for t in ROW_DOWN]

    def send_down():
        for t, layer, copy in down:
            ready(t, layer)
            copy.start()

    pl.when(a > 0)(send_down)

    def arrived(ref, sem):
        pltpu.make_async_copy(ref, ref, sem).wait()

    def product(t):
        lhs = jnp.concatenate([left[0, t], left[1, t]], axis=0)
        tiles = [
            jnp.concatenate([incoming[t, 0, j], incoming[t, 1, j]], axis=0)
            for j in range(tiles_of(t)[1])
        ]
        found = jnp.dot(
            lhs, jnp.concatenate(tiles, axis=1), preferred_element_type=jnp.float32
        )
        return [
            found[:, 2 * size * j : 2 * size * (j + 1)].reshape(2, size, 2 * size)
            for j in range(len(tiles))
        ]

    def receive(t):
        for layer in range(2):
            arrived(incoming.at[t, layer, pl.ds(0, tiles_of(t)[1])], recv_sems.at[t, layer])

    nothing = jnp.zeros((size, size), out_ref.dtype)

    def put(goal_a, goal_b, layer, block):
        place = 3 * STEPS.index((goal_a, goal_b)) + 1 + layer - z
        out_ref[0, place] = jnp.where(pattern[0, place] != 0, block, nothing)

    for j in range(5):
        incoming[CENTRE, z, j] = packed[z, j]
    arrived(left.at[other], left_sems.at[1])
    arrived(incoming.at[CENTRE, other], recv_sems.at[CENTRE, other])
    parts = product(CENTRE)
    blank = jnp.zeros((2, size, size), jnp.float32)
    for sb in range(3):
        total_low[sb] = parts[1 + sb]
    total_high[0] = jnp.concatenate([blank, parts[0][:, :, :size]], axis=2)
    total_high[1] = jnp.concatenate([blank, parts[0][:, :, size:]], axis=2)
    total_high[2] = jnp.concatenate([blank, parts[4][:, :, size:]], axis=2)
    for t in COLUMN:
        receive(t)
        parts = product(t)
        if t == 3:
            low, pair, at = parts[:2], parts[2], 0
        else:
            low, pair, at = parts[1:], parts[0], 1
        for i in range(2):
            total_low[at + i] += low[i]
        total_high[at] += jnp.concatenate([blank, pair[:, :, :size]], axis=2)
        total_high[at + 1] += jnp.concatenate([blank, pair[:, :, size:]], axis=2)

    def row_part(t, total):
        parts = product(t)
        at = {-1: 0, 0: 0, 1: 1}[STEPS[t][1]]
        for i, part in enumerate(parts):
            total[at + i] += part

    for t in ROW_DOWN:
        receive(t)
        row_part(t, total_high)
    for sb in range(3):
        total_low[sb] += jnp.concatenate([blank, total_high[sb][:, :, :size]], axis=2)
        ship[0, sb] = total_high[sb, other].astype(ship.dtype)

    copy_to(ship.at[0], landed.at[0], ship_sems.at[0, 0], ship_sems.at[0, 1], sibling).start()
    pl.when(a == 0)(send_down)

    for target in range(9):
        out_ref[0, 3 * target + 1 + z - other] = nothing
    for sb in range(3):
        own = total_high[sb, z].astype(out_ref.dtype)
        put(1, sb - 1, z, own[:, size:])
    arrived(landed.at[0], ship_sems.at[0, 1])
    for sb in range(3):
        put(1, sb - 1, other, landed[0, sb][:, size:])

    for t in ROW_UP:
        receive(t)
        row_part(t, total_low)
    for sb in range(3):
        ship[1, sb] = total_low[sb, other].astype(ship.dtype)
    copy_to(ship.at[1], landed.at[1], ship_sems.at[1, 0], ship_sems.at[1, 1], sibling).start()
    for sb in range(3):
        own = total_low[sb, z].astype(out_ref.dtype)
        put(-1, sb - 1, z, own[:, :size])
        put(0, sb - 1, z, own[:, size:])
    pl.when(jnp.logical_not(last_row))(sent_up)
    for copy in copies[len(up) : -1]:
        copy.wait_send()
    arrived(landed.at[1], ship_sems.at[1, 1])
    for sb in range(3):
        put(-1, sb - 1, other, landed[1, sb][:, :size])
        put(0, sb - 1, other, landed[1, sb][:, size:])
    copies[-1].wait_send()


def local(density, pattern):
    size = density.shape[-1]
    kind = density.dtype
    wide = 2 * size
    return pl.pallas_call(
        kernel,
        out_shape=jax.ShapeDtypeStruct(density.shape, kind),
        in_specs=[pl.BlockSpec(memory_space=pltpu.HBM)] * 2,
        out_specs=pl.BlockSpec(memory_space=pltpu.VMEM),
        scratch_shapes=[
            pltpu.VMEM((27, size, size), kind),
            pltpu.SMEM(pattern.shape, pattern.dtype),
            pltpu.VMEM((2, 9, size, size), kind),
            pltpu.VMEM((2, 9, size, wide), kind),
            pltpu.VMEM((2, len(TILES), size, wide), kind),
            pltpu.VMEM((9, 2, 5, size, wide), kind),
            pltpu.VMEM((3, 2, size, wide), jnp.float32),
            pltpu.VMEM((3, 2, size, wide), jnp.float32),
            pltpu.VMEM((2, 3, size, wide), kind),
            pltpu.VMEM((2, 3, size, wide), kind),
            pltpu.SemaphoreType.DMA((2,)),
            pltpu.SemaphoreType.REGULAR((9, 2)),
            pltpu.SemaphoreType.DMA((2,)),
            pltpu.SemaphoreType.DMA((9, 2)),
            pltpu.SemaphoreType.DMA((9, 2)),
            pltpu.SemaphoreType.DMA((2, 2)),
        ],
        compiler_params=pltpu.CompilerParams(
            collective_id=0,
            has_side_effects=True,
            vmem_limit_bytes=32 * 1024 * 1024,
        ),
    )(
        pltpu.with_memory_space_constraint(density, pltpu.HBM),
        pltpu.with_memory_space_constraint(pattern, pltpu.HBM),
    )


def solution(mesh):
    placed = (P(("row", "col", "depth"), None, None, None), P(("row", "col", "depth"), None))
    return jax.shard_map(
        local,
        mesh=mesh,
        in_specs=placed,
        out_specs=P(("row", "col", "depth"), None, None, None),
        check_vma=False,
    )
```

time: 35.4 us -> 32.2 us (0.910)
  local copies, waits for them, and re-layouts: 2.43 us -> 0.76 us
  Pallas kernels: 32.8 us -> 31.3 us
    unnamed x5 -> x1, local copies, waits for them, and re-layouts: 2.43 us -> 0.76 us
    pallas_call x1, Pallas kernels: 32.8 us -> 31.3 us  [local(): pl.pallas_call(kernel, out_shape=jax.ShapeDtypeStruct(density.shape, kind...]
where the time goes in v2:
time: 32.2 us; the launch traced here: 32.1 us
  Pallas kernels  31.3 us (97%)
  local copies, waits for them, and re-layouts  0.76 us (2%)
    pallas_call x1, Pallas kernels, local(): pl.pallas_call(kernel, out_shape=jax.ShapeDtypeStruct(density.shape, kind...  31.3 us
    unnamed x1, local copies, waits for them, and re-layouts  0.76 us

profile of v2, /device:TPU:1, one launch (start us, length us, event | category | flops | bytes accessed | tf_op | source)
XLA Modules:
  0.0 32.1 jit_solution(7005428358247344700)
XLA Ops:
  0.0 31.3 %shard_map.28 = bf16[1,27,64,64]{3,2,1,0:T(8,128)(2,1)S(1)} custom-call(bf16[1,27,64,64]{3,2,1,0:T(8,128)(2,1)} %density_hbm.1, s32[1,27]{1,0:T(1,128)} %pattern_hbm.1), custom_call_target="tpu_custom_call" | custom-call | tf_op jit(solution)/shard_map/pallas_call | solution.py:309
  31.3 0.8 %copy.4 = bf16[1,27,64,64]{3,2,1,0:T(8,128)(2,1)} copy(bf16[1,27,64,64]{3,2,1,0:T(8,128)(2,1)S(1)} %shard_map.28) | data formatting | bytes 442368

commit v3 on v2

--- a/solution.py
+++ b/solution.py
@@ -10,8 +10,9 @@
 CENTRE = 4
 ROW_UP = [0, 2, 1]
 COLUMN = [3, 5]
-ROW_DOWN = [6, 7, 8]
-AWAY = ROW_UP + COLUMN + ROW_DOWN
+ROW_DOWN = [7]
+SENT = ROW_UP + COLUMN + ROW_DOWN + [CENTRE]
+AWAY = [0, 1, 2, 3, 5, 6, 7, 8]
 
 TILES = [
     ((1, -1), (1, 0)),
@@ -49,6 +50,7 @@
     landed,
     load_sems,
     credits,
+    relay,
     left_sems,
     send_sems,
     recv_sems,
@@ -59,12 +61,17 @@
     other = 1 - z
     size = density.shape[-1]
 
-    loads = [
-        pltpu.make_async_copy(density_hbm.at[0], density, load_sems.at[0]),
-        pltpu.make_async_copy(pattern_hbm, pattern, load_sems.at[1]),
-    ]
-    for load in loads:
-        load.start()
+    def load(first, count, sem):
+        return pltpu.make_async_copy(
+            density_hbm.at[0, pl.ds(first, count), pl.ds(1 - z, 2)],
+            density.at[pl.ds(first, count)],
+            load_sems.at[sem],
+        )
+
+    load_pattern = pltpu.make_async_copy(pattern_hbm, pattern, load_sems.at[0])
+    load_first, load_rest = load(3, 6, 1), load(0, 3, 2)
+    for copy in (load_pattern, load_first, load_rest):
+        copy.start()
 
     def place_of(t, layer):
         step_a, step_b = STEPS[t]
@@ -78,17 +85,30 @@
         return dict(zip(("row", "col", "depth"), place_of(t, layer)))
 
     def rank(place):
-        index = (place[0] * cols + place[1]) * 2 + place[2]
-        return jnp.where(index == 0, 8 * cols - 1, 2 * index)
-
+        row, col, layer = place
+        inside = col * 2 + layer
+        index = row * 2 * cols + inside
+        late = jnp.where(row == rows - 1, 4 * cols + 1 + inside, 8 * cols + index)
+        return jnp.where(index == 0, 4 * cols, jnp.where(row < 2, index, late))
+
+    last_row = a == rows - 1
     mine = rank((a, b, z))
     partners = [(t, layer) for t in AWAY for layer in range(2)] + [(CENTRE, other)]
-    later = {}
+    direct = jnp.logical_not(last_row)
+    later, before = {}, {}
     for t, layer in partners:
-        later[t, 0 if t == CENTRE else layer] = rank(place_of(t, layer)) > mine
+        key = t, 0 if t == CENTRE else layer
+        after = rank(place_of(t, layer)) > mine
+        later[key], before[key] = after, jnp.logical_not(after)
+        if STEPS[t][0] == 0:
+            later[key] = jnp.logical_and(direct, after)
+            before[key] = jnp.logical_and(direct, jnp.logical_not(after))
 
     def is_later(t, layer):
         return later[t, 0 if t == CENTRE else layer]
+
+    def is_earlier(t, layer):
+        return before[t, 0 if t == CENTRE else layer]
 
     def credit(t, layer):
         return credits.at[t, 0 if t == CENTRE else layer]
@@ -96,7 +116,7 @@
     barrier = pltpu.get_barrier_semaphore()
     earlier = jnp.int32(0)
     for t, layer in partners:
-        earlier += jnp.where(is_later(t, layer), 0, 1)
+        earlier += jnp.where(is_earlier(t, layer), 1, 0)
 
         @pl.when(is_later(t, layer))
         def _(t=t, layer=layer):
@@ -108,9 +128,22 @@
     def _():
         pl.semaphore_wait(barrier, earlier)
 
+    def enter():
+        for t in ROW_UP:
+            for layer in range(2):
+                pl.semaphore_signal(
+                    relay.at[0], inc=1, device_id=device(t, layer), device_id_type=MESH
+                )
+
+    pl.when(last_row)(enter)
     for t, layer in partners:
-
-        @pl.when(jnp.logical_not(is_later(t, layer)))
+        if 8 - t not in SENT:
+            continue
+        credited = is_earlier(t, layer)
+        if t in ROW_UP:
+            credited = jnp.logical_and(direct, credited)
+
+        @pl.when(credited)
         def _(t=t, layer=layer):
             pl.semaphore_signal(
                 credits.at[8 - t, 0 if t == CENTRE else z],
@@ -152,7 +185,7 @@
         for slot in slots:
             for layer in range(2):
                 place = 3 * slot + 1 + layer - z
-                block = density[place]
+                block = density[slot, layer]
                 kept[layer, slot] = jnp.where(
                     pattern[0, place] != 0, block, jnp.zeros_like(block)
                 )
@@ -164,13 +197,12 @@
                     [kept[layer, STEPS.index(step)] for step in TILES[tile]], axis=1
                 )
 
-    for load in loads:
-        load.wait()
+    load_pattern.wait()
+    load_first.wait()
     keep(range(3, 9))
     pack(range(5, 8))
 
     up = [(t, layer, send(t, layer)) for t in ROW_UP for layer in range(2)]
-    last_row = a == rows - 1
 
     def send_up():
         for t, layer, copy in up:
@@ -182,30 +214,37 @@
             copy.wait_send()
 
     pl.when(last_row)(send_up)
+    load_rest.wait()
     keep(range(3))
     pack(range(5))
     for slot in range(9):
         left[z, slot] = jnp.concatenate([kept[0, slot], kept[1, slot]], axis=1)
-    pl.when(last_row)(sent_up)
-
-    for layer in (1, 0):
+
+    @pl.when(last_row)
+    def _():
+        sent_up()
+        pl.semaphore_wait(relay.at[1], 1)
+
+    def send_columns(layer):
         for t in COLUMN:
             ready(t, layer)
             send(t, layer).start()
+
+    send_columns(1)
+    pl.when(jnp.logical_not(last_row))(send_up)
     sibling = device(CENTRE, other)
     ready(CENTRE, other)
     copy_to(left.at[z], left.at[z], left_sems.at[0], left_sems.at[1], sibling).start()
     send(CENTRE, other).start()
-    pl.when(jnp.logical_not(last_row))(send_up)
+    send_columns(0)
 
     down = [(t, layer, send(t, layer)) for layer in (1, 0) for t in ROW_DOWN]
 
-    def send_down():
+    @pl.when(a > 0)
+    def _():
         for t, layer, copy in down:
             ready(t, layer)
             copy.start()
-
-    pl.when(a > 0)(send_down)
 
     def arrived(ref, sem):
         pltpu.make_async_copy(ref, ref, sem).wait()
@@ -233,6 +272,17 @@
     def put(goal_a, goal_b, layer, block):
         place = 3 * STEPS.index((goal_a, goal_b)) + 1 + layer - z
         out_ref[0, place] = jnp.where(pattern[0, place] != 0, block, nothing)
+
+    receive(7)
+    for corner, column, first in ((6, 3, 1), (8, 5, 0)):
+        for layer in range(2):
+            copy_to(
+                incoming.at[7, layer, pl.ds(first, 2)],
+                incoming.at[corner, layer, pl.ds(0, 2)],
+                send_sems.at[corner, layer],
+                recv_sems.at[corner, layer],
+                device(column, z),
+            ).start()
 
     for j in range(5):
         incoming[CENTRE, z, j] = packed[z, j]
@@ -263,7 +313,8 @@
         for i, part in enumerate(parts):
             total[at + i] += part
 
-    for t in ROW_DOWN:
+    row_part(7, total_high)
+    for t in (6, 8):
         receive(t)
         row_part(t, total_high)
     for sb in range(3):
@@ -271,7 +322,15 @@
         ship[0, sb] = total_high[sb, other].astype(ship.dtype)
 
     copy_to(ship.at[0], landed.at[0], ship_sems.at[0, 0], ship_sems.at[0, 1], sibling).start()
-    pl.when(a == 0)(send_down)
+
+    @pl.when(a == 0)
+    def _():
+        pl.semaphore_wait(relay.at[0], 6)
+        pl.semaphore_signal(
+            relay.at[1], inc=1, device_id=device(7, z), device_id_type=MESH
+        )
+        for _, _, copy in down:
+            copy.start()
 
     for target in range(9):
         out_ref[0, 3 * target + 1 + z - other] = nothing
@@ -312,7 +371,7 @@
         in_specs=[pl.BlockSpec(memory_space=pltpu.HBM)] * 2,
         out_specs=pl.BlockSpec(memory_space=pltpu.VMEM),
         scratch_shapes=[
-            pltpu.VMEM((27, size, size), kind),
+            pltpu.VMEM((9, 2, size, size), kind),
             pltpu.SMEM(pattern.shape, pattern.dtype),
             pltpu.VMEM((2, 9, size, size), kind),
             pltpu.VMEM((2, 9, size, wide), kind),
@@ -322,8 +381,9 @@
             pltpu.VMEM((3, 2, size, wide), jnp.float32),
             pltpu.VMEM((2, 3, size, wide), kind),
             pltpu.VMEM((2, 3, size, wide), kind),
-            pltpu.SemaphoreType.DMA((2,)),
+            pltpu.SemaphoreType.DMA((3,)),
             pltpu.SemaphoreType.REGULAR((9, 2)),
+            pltpu.SemaphoreType.REGULAR((2,)),
             pltpu.SemaphoreType.DMA((2,)),
             pltpu.SemaphoreType.DMA((9, 2)),
             pltpu.SemaphoreType.DMA((9, 2)),
@@ -335,7 +395,9 @@
             vmem_limit_bytes=32 * 1024 * 1024,
         ),
     )(
-        pltpu.with_memory_space_constraint(density, pltpu.HBM),
+        pltpu.with_memory_space_constraint(
+            density.reshape(1, 9, 3, size, size), pltpu.HBM
+        ),
         pltpu.with_memory_space_constraint(pattern, pltpu.HBM),
     )
 

time: 32.2 us -> 29.8 us (0.925)
  Pallas kernels: 31.3 us -> 28.9 us
    pallas_call x1, Pallas kernels: 31.3 us -> 28.9 us  [local(): pl.pallas_call(kernel, out_shape=jax.ShapeDtypeStruct(density.shape, kind...]
where the time goes in v3:
time: 29.8 us; the launch traced here: 29.7 us
  Pallas kernels  28.9 us (97%)
  local copies, waits for them, and re-layouts  0.76 us (3%)
    pallas_call x1, Pallas kernels, local(): pl.pallas_call(kernel, out_shape=jax.ShapeDtypeStruct(density.shape, kind...  28.9 us
    unnamed x1, local copies, waits for them, and re-layouts  0.76 us

profile of v3, /device:TPU:1, one launch (start us, length us, event | category | flops | bytes accessed | tf_op | source)
XLA Modules:
  0.0 29.7 jit_solution(9799972217271819915)
XLA Ops:
  0.0 28.9 %shard_map.28 = bf16[1,27,64,64]{3,2,1,0:T(8,128)(2,1)S(1)} custom-call(bf16[1,9,3,64,64]{4,3,2,1,0:T(8,128)(2,1)} %bitcast.1, s32[1,27]{1,0:T(1,128)} %pattern_hbm.1), custom_call_target="tpu_custom_call" | custom-call | tf_op jit(solution)/shard_map/pallas_call | solution.py:368
  28.9 0.8 %copy.4 = bf16[1,27,64,64]{3,2,1,0:T(8,128)(2,1)} copy(bf16[1,27,64,64]{3,2,1,0:T(8,128)(2,1)S(1)} %shard_map.28) | data formatting | bytes 442368

commit v4 on v3

--- a/solution.py
+++ b/solution.py
@@ -51,6 +51,12 @@
     load_sems,
     credits,
     relay,
+    extra,
+    staged,
+    partly,
+    extra_sems,
+    part_sems,
+    pass_sems,
     left_sems,
     send_sems,
     recv_sems,
@@ -69,40 +75,43 @@
         )
 
     load_pattern = pltpu.make_async_copy(pattern_hbm, pattern, load_sems.at[0])
-    load_first, load_rest = load(3, 6, 1), load(0, 3, 2)
-    for copy in (load_pattern, load_first, load_rest):
+    load_first, load_rest = [load(4, 2, 1), load(7, 2, 2)], [load(3, 1, 3), load(6, 1, 4), load(0, 3, 5)]
+    for copy in [load_pattern] + load_first + load_rest:
         copy.start()
 
-    def place_of(t, layer):
+    last, end = rows - 1, cols - 1
+    last_row, first_row = a == last, a == 0
+    meeting = first_row & (b == 0)
+    row_of = {-1: jnp.where(last_row, 0, a + 1), 0: a, 1: jnp.where(first_row, last, a - 1)}
+    col_of = {-1: jnp.where(b == end, 0, b + 1), 0: b, 1: jnp.where(b == 0, end, b - 1)}
+
+    def device(t, layer):
         step_a, step_b = STEPS[t]
-        return (
-            lax.rem(a - step_a + rows, rows),
-            lax.rem(b - step_b + cols, cols),
-            layer,
-        )
-
-    def device(t, layer):
-        return dict(zip(("row", "col", "depth"), place_of(t, layer)))
-
-    def rank(place):
-        row, col, layer = place
-        inside = col * 2 + layer
-        index = row * 2 * cols + inside
-        late = jnp.where(row == rows - 1, 4 * cols + 1 + inside, 8 * cols + index)
-        return jnp.where(index == 0, 4 * cols, jnp.where(row < 2, index, late))
-
-    last_row = a == rows - 1
-    mine = rank((a, b, z))
+        return {"row": row_of[step_a], "col": col_of[step_b], "depth": layer}
+
     partners = [(t, layer) for t in AWAY for layer in range(2)] + [(CENTRE, other)]
     direct = jnp.logical_not(last_row)
-    later, before = {}, {}
+    is_first = first_row & (b == 0) & (z == 0)
+    row_later = {
+        -1: direct & (a != last - 1 if rows > 3 else a < last) & jnp.logical_not(is_first),
+        1: first_row | last_row if rows > 3 else first_row,
+    }
+    col_later = {-1: b != end, 0: z == 0, 1: b == 0}
+    later, before, late = {}, {}, {}
     for t, layer in partners:
+        step_a, step_b = STEPS[t]
         key = t, 0 if t == CENTRE else layer
-        after = rank(place_of(t, layer)) > mine
-        later[key], before[key] = after, jnp.logical_not(after)
-        if STEPS[t][0] == 0:
-            later[key] = jnp.logical_and(direct, after)
-            before[key] = jnp.logical_and(direct, jnp.logical_not(after))
+        to_first = jnp.bool_(False)
+        if step_a == 1 or step_a == 0:
+            to_first = (row_of[step_a] == 0) & (col_of[step_b] == 0)
+            to_first = to_first & (layer == 0)
+        if step_a == 0:
+            after = direct & ((col_later[step_b] & jnp.logical_not(is_first)) | to_first)
+            ahead = direct & jnp.logical_not(after)
+        else:
+            after = row_later[step_a] | to_first
+            ahead = jnp.logical_not(after)
+        later[key], before[key], late[key] = after, ahead, to_first
 
     def is_later(t, layer):
         return later[t, 0 if t == CENTRE else layer]
@@ -114,43 +123,53 @@
         return credits.at[t, 0 if t == CENTRE else layer]
 
     barrier = pltpu.get_barrier_semaphore()
-    earlier = jnp.int32(0)
-    for t, layer in partners:
-        earlier += jnp.where(is_earlier(t, layer), 1, 0)
-
-        @pl.when(is_later(t, layer))
-        def _(t=t, layer=layer):
-            pl.semaphore_signal(
-                barrier, inc=1, device_id=device(t, layer), device_id_type=MESH
-            )
-
-    @pl.when(earlier > 0)
-    def _():
-        pl.semaphore_wait(barrier, earlier)
-
-    def enter():
+
+    def greet():
+        for t, layer in partners:
+
+            @pl.when(is_later(t, layer))
+            def _(t=t, layer=layer):
+                pl.semaphore_signal(
+                    barrier, inc=1, device_id=device(t, layer), device_id_type=MESH
+                )
+
+    def meet():
+        earlier = jnp.int32(0)
+        for t, layer in partners:
+            earlier += is_earlier(t, layer).astype(jnp.int32)
+
+        @pl.when(earlier > 0)
+        def _():
+            pl.semaphore_wait(barrier, earlier)
+
+    @pl.when(direct)
+    def _():
+        greet()
+        meet()
+        for t, layer in partners:
+            if 8 - t not in SENT:
+                continue
+
+            @pl.when(is_earlier(t, layer))
+            def _(t=t, layer=layer):
+                pl.semaphore_signal(
+                    credits.at[8 - t, 0 if t == CENTRE else z],
+                    inc=1,
+                    device_id=device(t, layer),
+                    device_id_type=MESH,
+                )
+
+    @pl.when(last_row)
+    def _():
+        meet()
         for t in ROW_UP:
             for layer in range(2):
                 pl.semaphore_signal(
-                    relay.at[0], inc=1, device_id=device(t, layer), device_id_type=MESH
+                    relay.at[0 if t == 1 else 1],
+                    inc=1,
+                    device_id=device(t, layer),
+                    device_id_type=MESH,
                 )
-
-    pl.when(last_row)(enter)
-    for t, layer in partners:
-        if 8 - t not in SENT:
-            continue
-        credited = is_earlier(t, layer)
-        if t in ROW_UP:
-            credited = jnp.logical_and(direct, credited)
-
-        @pl.when(credited)
-        def _(t=t, layer=layer):
-            pl.semaphore_signal(
-                credits.at[8 - t, 0 if t == CENTRE else z],
-                inc=1,
-                device_id=device(t, layer),
-                device_id_type=MESH,
-            )
 
     def ready(t, layer):
         @pl.when(is_later(t, layer))
@@ -198,23 +217,51 @@
                 )
 
     load_pattern.wait()
-    load_first.wait()
-    keep(range(3, 9))
-    pack(range(5, 8))
-
-    up = [(t, layer, send(t, layer)) for t in ROW_UP for layer in range(2)]
-
-    def send_up():
-        for t, layer, copy in up:
+    for copy in load_first:
+        copy.wait()
+    keep((4, 5, 7, 8))
+    pack((6, 7))
+
+    up = [(t, layer, send(t, layer)) for t in ROW_UP for layer in (1, 0)]
+    around = [
+        copy_to(
+            packed.at[1 - layer, pl.ds(6, 2)],
+            extra.at[z],
+            pass_sems.at[layer],
+            extra_sems.at[z],
+            device(0, layer),
+        )
+        for layer in range(2)
+    ]
+    far = last_row & (b == end)
+
+    def send_up(messages=up):
+        for t, layer, copy in messages:
             ready(t, layer)
             copy.start()
+            if t == 0:
+                pl.when(far)(around[layer].start)
 
     def sent_up():
         for _, _, copy in up:
             copy.wait_send()
 
-    pl.when(last_row)(send_up)
-    load_rest.wait()
+        @pl.when(far)
+        def _():
+            for copy in around:
+                copy.wait_send()
+
+    pl.when(last_row)(lambda: send_up(up[:2]))
+    for copy in load_rest:
+        copy.wait()
+    keep((3, 6))
+    pack((5,))
+
+    @pl.when(last_row)
+    def _():
+        send_up(up[2:])
+        greet()
+
     keep(range(3))
     pack(range(5))
     for slot in range(9):
@@ -223,28 +270,32 @@
     @pl.when(last_row)
     def _():
         sent_up()
-        pl.semaphore_wait(relay.at[1], 1)
-
-    def send_columns(layer):
-        for t in COLUMN:
-            ready(t, layer)
-            send(t, layer).start()
-
-    send_columns(1)
-    pl.when(jnp.logical_not(last_row))(send_up)
+        pl.semaphore_wait(relay.at[2], 1)
+
     sibling = device(CENTRE, other)
-    ready(CENTRE, other)
-    copy_to(left.at[z], left.at[z], left_sems.at[0], left_sems.at[1], sibling).start()
-    send(CENTRE, other).start()
-    send_columns(0)
-
-    down = [(t, layer, send(t, layer)) for layer in (1, 0) for t in ROW_DOWN]
-
-    @pl.when(a > 0)
-    def _():
-        for t, layer, copy in down:
-            ready(t, layer)
-            copy.start()
+    swap = copy_to(left.at[z], left.at[z], left_sems.at[0], left_sems.at[1], sibling)
+    near = [(t, layer, [send(t, layer)]) for t in COLUMN for layer in range(2)]
+    near.append((CENTRE, other, [swap, send(CENTRE, other)]))
+    down = [(t, layer, send(t, layer)) for t in ROW_DOWN for layer in range(2)]
+
+    def offer(messages, wanted):
+        for t, layer, group in messages:
+
+            @pl.when(wanted(t, layer))
+            def _(t=t, layer=layer, group=group):
+                ready(t, layer)
+                for copy in group:
+                    copy.start()
+
+    def to_first(t, layer):
+        return late[t, 0 if t == CENTRE else layer]
+
+    downward = [(t, layer, [copy]) for t, layer, copy in down]
+    offer(near, lambda t, layer: jnp.logical_not(to_first(t, layer)))
+    offer(downward, lambda t, layer: (a > 0) & jnp.logical_not(to_first(t, layer)))
+    pl.when(direct)(send_up)
+    offer([m for m in near if m[0] == CENTRE or m[1] == 0], to_first)
+    offer(downward[:1], lambda t, layer: (a > 0) & to_first(t, layer))
 
     def arrived(ref, sem):
         pltpu.make_async_copy(ref, ref, sem).wait()
@@ -325,10 +376,7 @@
 
     @pl.when(a == 0)
     def _():
-        pl.semaphore_wait(relay.at[0], 6)
-        pl.semaphore_signal(
-            relay.at[1], inc=1, device_id=device(7, z), device_id_type=MESH
-        )
+        pl.semaphore_wait(relay.at[0], 2)
         for _, _, copy in down:
             copy.start()
 
@@ -337,28 +385,72 @@
     for sb in range(3):
         own = total_high[sb, z].astype(out_ref.dtype)
         put(1, sb - 1, z, own[:, size:])
-    arrived(landed.at[0], ship_sems.at[0, 1])
-    for sb in range(3):
-        put(1, sb - 1, other, landed[0, sb][:, size:])
-
-    for t in ROW_UP:
+
+    sent = copies[len(up) + len(around) :]
+
+    def take(t):
         receive(t)
         row_part(t, total_low)
+
+    @pl.when(first_row)
+    def _():
+        pl.semaphore_wait(relay.at[1], 4)
+        pl.semaphore_signal(
+            relay.at[2], inc=1, device_id=device(7, z), device_id_type=MESH
+        )
+
+    pl.when(jnp.logical_not(meeting))(lambda: take(0))
+    take(2)
+    take(1)
+    partial = copy_to(staged, partly, part_sems.at[0], part_sems.at[1], sibling)
+    swap_last = copy_to(
+        ship.at[1], landed.at[1], ship_sems.at[1, 0], ship_sems.at[1, 1], sibling
+    )
+
+    @pl.when(meeting)
+    def _():
+        for sb in range(3):
+            staged[sb] = total_low[sb, other]
+        partial.start()
+        arrived(partly, part_sems.at[1])
+        for layer in range(2):
+            arrived(extra.at[layer], extra_sems.at[layer])
+        found = jnp.dot(
+            left[z, 0],
+            jnp.concatenate(
+                [jnp.concatenate([extra[0, j], extra[1, j]], axis=0) for j in range(2)], axis=1
+            ),
+            preferred_element_type=jnp.float32,
+        )
+        for sb in range(3):
+            whole = partly[sb]
+            if sb < 2:
+                whole += found[:, 2 * size * sb : 2 * size * (sb + 1)]
+            landed[1, sb] = whole.astype(landed.dtype)
+        take(0)
+
     for sb in range(3):
         ship[1, sb] = total_low[sb, other].astype(ship.dtype)
-    copy_to(ship.at[1], landed.at[1], ship_sems.at[1, 0], ship_sems.at[1, 1], sibling).start()
+
+    pl.when(jnp.logical_not(meeting))(swap_last.start)
+    arrived(landed.at[0], ship_sems.at[0, 1])
+    for sb in range(3):
+        put(1, sb - 1, other, landed[0, sb][:, size:])
+
     for sb in range(3):
         own = total_low[sb, z].astype(out_ref.dtype)
         put(-1, sb - 1, z, own[:, :size])
         put(0, sb - 1, z, own[:, size:])
     pl.when(jnp.logical_not(last_row))(sent_up)
-    for copy in copies[len(up) : -1]:
+    for copy in sent:
         copy.wait_send()
-    arrived(landed.at[1], ship_sems.at[1, 1])
+
+    pl.when(meeting)(partial.wait_send)
+    pl.when(jnp.logical_not(meeting))(lambda: arrived(landed.at[1], ship_sems.at[1, 1]))
     for sb in range(3):
         put(-1, sb - 1, other, landed[1, sb][:, :size])
         put(0, sb - 1, other, landed[1, sb][:, size:])
-    copies[-1].wait_send()
+    pl.when(jnp.logical_not(meeting))(swap_last.wait_send)
 
 
 def local(density, pattern):
@@ -381,9 +473,15 @@
             pltpu.VMEM((3, 2, size, wide), jnp.float32),
             pltpu.VMEM((2, 3, size, wide), kind),
             pltpu.VMEM((2, 3, size, wide), kind),
-            pltpu.SemaphoreType.DMA((3,)),
+            pltpu.SemaphoreType.DMA((6,)),
             pltpu.SemaphoreType.REGULAR((9, 2)),
-            pltpu.SemaphoreType.REGULAR((2,)),
+            pltpu.SemaphoreType.REGULAR((3,)),
+            pltpu.VMEM((2, 2, size, wide), kind),
+            pltpu.VMEM((3, size, wide), jnp.float32),
+            pltpu.VMEM((3, size, wide), jnp.float32),
+            pltpu.SemaphoreType.DMA((2,)),
+            pltpu.SemaphoreType.DMA((2,)),
+            pltpu.SemaphoreType.DMA((2,)),
             pltpu.SemaphoreType.DMA((2,)),
             pltpu.SemaphoreType.DMA((9, 2)),
             pltpu.SemaphoreType.DMA((9, 2)),

time: 29.8 us -> 29.1 us (0.977)
  Pallas kernels: 28.9 us -> 28.1 us
    pallas_call x1, Pallas kernels: 28.9 us -> 28.1 us  [local(): pl.pallas_call(kernel, out_shape=jax.ShapeDtypeStruct(density.shape, kind...]
where the time goes in v4:
time: 29.1 us; the launch traced here: 28.9 us
  Pallas kernels  28.1 us (97%)
  local copies, waits for them, and re-layouts  0.76 us (3%)
    pallas_call x1, Pallas kernels, local(): pl.pallas_call(kernel, out_shape=jax.ShapeDtypeStruct(density.shape, kind...  28.1 us
    unnamed x1, local copies, waits for them, and re-layouts  0.76 us

profile of v4, /device:TPU:1, one launch (start us, length us, event | category | flops | bytes accessed | tf_op | source)
XLA Modules:
  0.0 28.9 jit_solution(12363013526604425572)
XLA Ops:
  0.0 28.1 %shard_map.28 = bf16[1,27,64,64]{3,2,1,0:T(8,128)(2,1)S(1)} custom-call(bf16[1,9,3,64,64]{4,3,2,1,0:T(8,128)(2,1)} %bitcast.1, s32[1,27]{1,0:T(1,128)} %pattern_hbm.1), custom_call_target="tpu_custom_call" | custom-call | tf_op jit(solution)/shard_map/pallas_call | solution.py:460
  28.2 0.8 %copy.4 = bf16[1,27,64,64]{3,2,1,0:T(8,128)(2,1)} copy(bf16[1,27,64,64]{3,2,1,0:T(8,128)(2,1)S(1)} %shard_map.28) | data formatting | bytes 442368

commit v5 on v4

--- a/solution.py
+++ b/solution.py
@@ -54,9 +54,9 @@
     extra,
     staged,
     partly,
-    extra_sems,
+    extra_sem,
     part_sems,
-    pass_sems,
+    around_sem,
     left_sems,
     send_sems,
     recv_sems,
@@ -75,8 +75,8 @@
         )
 
     load_pattern = pltpu.make_async_copy(pattern_hbm, pattern, load_sems.at[0])
-    load_first, load_rest = [load(4, 2, 1), load(7, 2, 2)], [load(3, 1, 3), load(6, 1, 4), load(0, 3, 5)]
-    for copy in [load_pattern] + load_first + load_rest:
+    load_first, load_rest = load(4, 5, 1), load(0, 4, 2)
+    for copy in (load_pattern, load_first, load_rest):
         copy.start()
 
     last, end = rows - 1, cols - 1
@@ -120,7 +120,10 @@
         return before[t, 0 if t == CENTRE else layer]
 
     def credit(t, layer):
-        return credits.at[t, 0 if t == CENTRE else layer]
+        base = {3: 1, 5: 3, 7: 6}
+        if t in ROW_UP:
+            return credits.at[0]
+        return credits.at[5 if t == CENTRE else base[t] + layer]
 
     barrier = pltpu.get_barrier_semaphore()
 
@@ -153,7 +156,7 @@
             @pl.when(is_earlier(t, layer))
             def _(t=t, layer=layer):
                 pl.semaphore_signal(
-                    credits.at[8 - t, 0 if t == CENTRE else z],
+                    credit(8 - t, z),
                     inc=1,
                     device_id=device(t, layer),
                     device_id_type=MESH,
@@ -176,10 +179,8 @@
         def _():
             pl.semaphore_wait(credit(t, layer), 1)
 
-    copies = []
-
     def copy_to(src, dst, send_sem, recv_sem, target):
-        copy = pltpu.make_async_remote_copy(
+        return pltpu.make_async_remote_copy(
             src_ref=src,
             dst_ref=dst,
             send_sem=send_sem,
@@ -187,16 +188,14 @@
             device_id=target,
             device_id_type=MESH,
         )
-        copies.append(copy)
-        return copy
 
     def send(t, layer):
         first, count = tiles_of(t)
         return copy_to(
             packed.at[layer, pl.ds(first, count)],
             incoming.at[t, z, pl.ds(0, count)],
-            send_sems.at[t, 0 if t == CENTRE else layer],
-            recv_sems.at[t, z],
+            send_sems.at[t],
+            recv_sems.at[t],
             device(t, layer),
         )
 
@@ -217,8 +216,7 @@
                 )
 
     load_pattern.wait()
-    for copy in load_first:
-        copy.wait()
+    load_first.wait()
     keep((4, 5, 7, 8))
     pack((6, 7))
 
@@ -227,8 +225,8 @@
         copy_to(
             packed.at[1 - layer, pl.ds(6, 2)],
             extra.at[z],
-            pass_sems.at[layer],
-            extra_sems.at[z],
+            around_sem,
+            extra_sem,
             device(0, layer),
         )
         for layer in range(2)
@@ -237,29 +235,30 @@
 
     def send_up(messages=up):
         for t, layer, copy in messages:
-            ready(t, layer)
             copy.start()
             if t == 0:
                 pl.when(far)(around[layer].start)
 
+    def arrived(ref, sem):
+        pltpu.make_async_copy(ref, ref, sem).wait()
+
+    def sent(t):
+        first, count = tiles_of(t)
+        arrived(packed.at[:, pl.ds(first, count)], send_sems.at[t])
+
     def sent_up():
-        for _, _, copy in up:
-            copy.wait_send()
-
-        @pl.when(far)
-        def _():
-            for copy in around:
-                copy.wait_send()
-
-    pl.when(last_row)(lambda: send_up(up[:2]))
-    for copy in load_rest:
-        copy.wait()
+        for t in ROW_UP:
+            sent(t)
+        pl.when(far)(lambda: arrived(packed.at[:, pl.ds(6, 2)], around_sem))
+
+    pl.when(last_row)(lambda: send_up(up[:1]))
+    load_rest.wait()
     keep((3, 6))
     pack((5,))
 
     @pl.when(last_row)
     def _():
-        send_up(up[2:])
+        pl.when(jnp.logical_not(far))(lambda: send_up(up[1:]))
         greet()
 
     keep(range(3))
@@ -267,6 +266,8 @@
     for slot in range(9):
         left[z, slot] = jnp.concatenate([kept[0, slot], kept[1, slot]], axis=1)
 
+    pl.when(far)(lambda: send_up(up[1:]))
+
     @pl.when(last_row)
     def _():
         sent_up()
@@ -275,7 +276,8 @@
     sibling = device(CENTRE, other)
     swap = copy_to(left.at[z], left.at[z], left_sems.at[0], left_sems.at[1], sibling)
     near = [(t, layer, [send(t, layer)]) for t in COLUMN for layer in range(2)]
-    near.append((CENTRE, other, [swap, send(CENTRE, other)]))
+    centre = send(CENTRE, other)
+    near.append((CENTRE, other, [swap, centre]))
     down = [(t, layer, send(t, layer)) for t in ROW_DOWN for layer in range(2)]
 
     def offer(messages, wanted):
@@ -293,12 +295,21 @@
     downward = [(t, layer, [copy]) for t, layer, copy in down]
     offer(near, lambda t, layer: jnp.logical_not(to_first(t, layer)))
     offer(downward, lambda t, layer: (a > 0) & jnp.logical_not(to_first(t, layer)))
-    pl.when(direct)(send_up)
+
+    @pl.when(direct)
+    def _():
+        awaited = jnp.int32(0)
+        for t, layer, _ in up:
+            awaited += is_later(t, layer).astype(jnp.int32)
+
+        @pl.when(awaited > 0)
+        def _():
+            pl.semaphore_wait(credits.at[0], awaited)
+
+        send_up()
+
     offer([m for m in near if m[0] == CENTRE or m[1] == 0], to_first)
     offer(downward[:1], lambda t, layer: (a > 0) & to_first(t, layer))
-
-    def arrived(ref, sem):
-        pltpu.make_async_copy(ref, ref, sem).wait()
 
     def product(t):
         lhs = jnp.concatenate([left[0, t], left[1, t]], axis=0)
@@ -315,8 +326,7 @@
         ]
 
     def receive(t):
-        for layer in range(2):
-            arrived(incoming.at[t, layer, pl.ds(0, tiles_of(t)[1])], recv_sems.at[t, layer])
+        arrived(incoming.at[t, :, pl.ds(0, tiles_of(t)[1])], recv_sems.at[t])
 
     nothing = jnp.zeros((size, size), out_ref.dtype)
 
@@ -325,20 +335,23 @@
         out_ref[0, place] = jnp.where(pattern[0, place] != 0, block, nothing)
 
     receive(7)
-    for corner, column, first in ((6, 3, 1), (8, 5, 0)):
-        for layer in range(2):
-            copy_to(
-                incoming.at[7, layer, pl.ds(first, 2)],
-                incoming.at[corner, layer, pl.ds(0, 2)],
-                send_sems.at[corner, layer],
-                recv_sems.at[corner, layer],
-                device(column, z),
-            ).start()
+    onward = [
+        copy_to(
+            incoming.at[7, :, pl.ds(first, 2)],
+            incoming.at[corner, :, pl.ds(0, 2)],
+            send_sems.at[corner],
+            recv_sems.at[corner],
+            device(column, z),
+        )
+        for corner, column, first in ((6, 3, 1), (8, 5, 0))
+    ]
+    for copy in onward:
+        copy.start()
 
     for j in range(5):
         incoming[CENTRE, z, j] = packed[z, j]
     arrived(left.at[other], left_sems.at[1])
-    arrived(incoming.at[CENTRE, other], recv_sems.at[CENTRE, other])
+    arrived(incoming.at[CENTRE, other], recv_sems.at[CENTRE])
     parts = product(CENTRE)
     blank = jnp.zeros((2, size, size), jnp.float32)
     for sb in range(3):
@@ -372,7 +385,10 @@
         total_low[sb] += jnp.concatenate([blank, total_high[sb][:, :, :size]], axis=2)
         ship[0, sb] = total_high[sb, other].astype(ship.dtype)
 
-    copy_to(ship.at[0], landed.at[0], ship_sems.at[0, 0], ship_sems.at[0, 1], sibling).start()
+    swap_first = copy_to(
+        ship.at[0], landed.at[0], ship_sems.at[0, 0], ship_sems.at[0, 1], sibling
+    )
+    swap_first.start()
 
     @pl.when(a == 0)
     def _():
@@ -386,8 +402,6 @@
         own = total_high[sb, z].astype(out_ref.dtype)
         put(1, sb - 1, z, own[:, size:])
 
-    sent = copies[len(up) + len(around) :]
-
     def take(t):
         receive(t)
         row_part(t, total_low)
@@ -402,6 +416,17 @@
     pl.when(jnp.logical_not(meeting))(lambda: take(0))
     take(2)
     take(1)
+
+    def tidy():
+        arrived(landed.at[0], ship_sems.at[0, 1])
+        for sb in range(3):
+            put(1, sb - 1, other, landed[0, sb][:, size:])
+        pl.when(jnp.logical_not(last_row))(sent_up)
+        for t in COLUMN + ROW_DOWN:
+            sent(t)
+        for copy in [swap, centre, swap_first] + onward:
+            copy.wait_send()
+
     partial = copy_to(staged, partly, part_sems.at[0], part_sems.at[1], sibling)
     swap_last = copy_to(
         ship.at[1], landed.at[1], ship_sems.at[1, 0], ship_sems.at[1, 1], sibling
@@ -412,9 +437,9 @@
         for sb in range(3):
             staged[sb] = total_low[sb, other]
         partial.start()
+        tidy()
         arrived(partly, part_sems.at[1])
-        for layer in range(2):
-            arrived(extra.at[layer], extra_sems.at[layer])
+        arrived(extra, extra_sem)
         found = jnp.dot(
             left[z, 0],
             jnp.concatenate(
@@ -432,19 +457,16 @@
     for sb in range(3):
         ship[1, sb] = total_low[sb, other].astype(ship.dtype)
 
-    pl.when(jnp.logical_not(meeting))(swap_last.start)
-    arrived(landed.at[0], ship_sems.at[0, 1])
-    for sb in range(3):
-        put(1, sb - 1, other, landed[0, sb][:, size:])
+
+    @pl.when(jnp.logical_not(meeting))
+    def _():
+        swap_last.start()
+        tidy()
 
     for sb in range(3):
         own = total_low[sb, z].astype(out_ref.dtype)
         put(-1, sb - 1, z, own[:, :size])
         put(0, sb - 1, z, own[:, size:])
-    pl.when(jnp.logical_not(last_row))(sent_up)
-    for copy in sent:
-        copy.wait_send()
-
     pl.when(meeting)(partial.wait_send)
     pl.when(jnp.logical_not(meeting))(lambda: arrived(landed.at[1], ship_sems.at[1, 1]))
     for sb in range(3):
@@ -473,18 +495,18 @@
             pltpu.VMEM((3, 2, size, wide), jnp.float32),
             pltpu.VMEM((2, 3, size, wide), kind),
             pltpu.VMEM((2, 3, size, wide), kind),
-            pltpu.SemaphoreType.DMA((6,)),
-            pltpu.SemaphoreType.REGULAR((9, 2)),
+            pltpu.SemaphoreType.DMA((3,)),
+            pltpu.SemaphoreType.REGULAR((8,)),
             pltpu.SemaphoreType.REGULAR((3,)),
             pltpu.VMEM((2, 2, size, wide), kind),
             pltpu.VMEM((3, size, wide), jnp.float32),
             pltpu.VMEM((3, size, wide), jnp.float32),
+            pltpu.SemaphoreType.DMA,
             pltpu.SemaphoreType.DMA((2,)),
+            pltpu.SemaphoreType.DMA,
             pltpu.SemaphoreType.DMA((2,)),
-            pltpu.SemaphoreType.DMA((2,)),
-            pltpu.SemaphoreType.DMA((2,)),
-            pltpu.SemaphoreType.DMA((9, 2)),
-            pltpu.SemaphoreType.DMA((9, 2)),
+            pltpu.SemaphoreType.DMA((9,)),
+            pltpu.SemaphoreType.DMA((9,)),
             pltpu.SemaphoreType.DMA((2, 2)),
         ],
         compiler_params=pltpu.CompilerParams(

time: 29.1 us -> 28.7 us (0.986)
  Pallas kernels: 28.1 us -> 27.8 us
    pallas_call x1, Pallas kernels: 28.1 us -> 27.8 us  [local(): pl.pallas_call(kernel, out_shape=jax.ShapeDtypeStruct(density.shape, kind...]
where the time goes in v5:
time: 28.7 us; the launch traced here: 28.6 us
  Pallas kernels  27.8 us (97%)
  local copies, waits for them, and re-layouts  0.76 us (3%)
    pallas_call x1, Pallas kernels, local(): pl.pallas_call(kernel, out_shape=jax.ShapeDtypeStruct(density.shape, kind...  27.8 us
    unnamed x1, local copies, waits for them, and re-layouts  0.76 us

profile of v5, /device:TPU:1, one launch (start us, length us, event | category | flops | bytes accessed | tf_op | source)
XLA Modules:
  0.0 28.6 jit_solution(13092449543565728618)
XLA Ops:
  0.0 27.8 %shard_map.28 = bf16[1,27,64,64]{3,2,1,0:T(8,128)(2,1)S(1)} custom-call(bf16[1,9,3,64,64]{4,3,2,1,0:T(8,128)(2,1)} %bitcast.1, s32[1,27]{1,0:T(1,128)} %pattern_hbm.1), custom_call_target="tpu_custom_call" | custom-call | tf_op jit(solution)/shard_map/pallas_call | solution.py:482
  27.8 0.8 %copy.4 = bf16[1,27,64,64]{3,2,1,0:T(8,128)(2,1)} copy(bf16[1,27,64,64]{3,2,1,0:T(8,128)(2,1)S(1)} %shard_map.28) | data formatting | bytes 442368

commit v6 on v5

--- a/solution.py
+++ b/solution.py
@@ -266,7 +266,7 @@
     for slot in range(9):
         left[z, slot] = jnp.concatenate([kept[0, slot], kept[1, slot]], axis=1)
 
-    pl.when(far)(lambda: send_up(up[1:]))
+    pl.when(far)(lambda: send_up(up[2:] + up[1:2]))
 
     @pl.when(last_row)
     def _():
@@ -440,6 +440,7 @@
         tidy()
         arrived(partly, part_sems.at[1])
         arrived(extra, extra_sem)
+        receive(0)
         found = jnp.dot(
             left[z, 0],
             jnp.concatenate(
@@ -452,7 +453,7 @@
             if sb < 2:
                 whole += found[:, 2 * size * sb : 2 * size * (sb + 1)]
             landed[1, sb] = whole.astype(landed.dtype)
-        take(0)
+        row_part(0, total_low)
 
     for sb in range(3):
         ship[1, sb] = total_low[sb, other].astype(ship.dtype)

time: 28.7 us -> 28.6 us (level)
  no operation moved by 1% of the time
where the time goes in v6:
time: 28.6 us; the launch traced here: 28.4 us
  Pallas kernels  27.6 us (97%)
  local copies, waits for them, and re-layouts  0.76 us (3%)
    pallas_call x1, Pallas kernels, local(): pl.pallas_call(kernel, out_shape=jax.ShapeDtypeStruct(density.shape, kind...  27.6 us
    unnamed x1, local copies, waits for them, and re-layouts  0.76 us

profile of v6, /device:TPU:1, one launch (start us, length us, event | category | flops | bytes accessed | tf_op | source)
XLA Modules:
  0.0 28.4 jit_solution(4679638437340622156)
XLA Ops:
  0.0 27.6 %shard_map.28 = bf16[1,27,64,64]{3,2,1,0:T(8,128)(2,1)S(1)} custom-call(bf16[1,9,3,64,64]{4,3,2,1,0:T(8,128)(2,1)} %bitcast.1, s32[1,27]{1,0:T(1,128)} %pattern_hbm.1), custom_call_target="tpu_custom_call" | custom-call | tf_op jit(solution)/shard_map/pallas_call | solution.py:483
  27.7 0.8 %copy.4 = bf16[1,27,64,64]{3,2,1,0:T(8,128)(2,1)} copy(bf16[1,27,64,64]{3,2,1,0:T(8,128)(2,1)S(1)} %shard_map.28) | data formatting | bytes 442368

commit v7 on v6

--- a/solution.py
+++ b/solution.py
@@ -75,8 +75,8 @@
         )
 
     load_pattern = pltpu.make_async_copy(pattern_hbm, pattern, load_sems.at[0])
-    load_first, load_rest = load(4, 5, 1), load(0, 4, 2)
-    for copy in (load_pattern, load_first, load_rest):
+    load_first = [load(4, 2, 1), load(7, 2, 1)]
+    for copy in [load_pattern] + load_first:
         copy.start()
 
     last, end = rows - 1, cols - 1
@@ -216,7 +216,11 @@
                 )
 
     load_pattern.wait()
-    load_first.wait()
+    whole = density.at[pl.ds(0, 4)]
+    pltpu.make_async_copy(whole, whole, load_sems.at[1]).wait()
+    load_rest = [load(3, 1, 2), load(6, 1, 2), load(0, 3, 2)]
+    for copy in load_rest:
+        copy.start()
     keep((4, 5, 7, 8))
     pack((6, 7))
 
@@ -252,7 +256,8 @@
         pl.when(far)(lambda: arrived(packed.at[:, pl.ds(6, 2)], around_sem))
 
     pl.when(last_row)(lambda: send_up(up[:1]))
-    load_rest.wait()
+    whole = density.at[pl.ds(0, 5)]
+    pltpu.make_async_copy(whole, whole, load_sems.at[2]).wait()
     keep((3, 6))
     pack((5,))
 

time: 28.6 us -> 28.4 us (level)
  no operation moved by 1% of the time
where the time goes in v7:
time: 28.4 us; the launch traced here: 28.1 us
  Pallas kernels  27.4 us (96%)
  local copies, waits for them, and re-layouts  0.76 us (3%)
    pallas_call x1, Pallas kernels, local(): pl.pallas_call(kernel, out_shape=jax.ShapeDtypeStruct(density.shape, kind...  27.4 us
    unnamed x1, local copies, waits for them, and re-layouts  0.76 us

profile of v7, /device:TPU:1, one launch (start us, length us, event | category | flops | bytes accessed | tf_op | source)
XLA Modules:
  0.0 28.1 jit_solution(16840189682331543987)
XLA Ops:
  0.0 27.4 %shard_map.28 = bf16[1,27,64,64]{3,2,1,0:T(8,128)(2,1)S(1)} custom-call(bf16[1,9,3,64,64]{4,3,2,1,0:T(8,128)(2,1)} %bitcast.1, s32[1,27]{1,0:T(1,128)} %pattern_hbm.1), custom_call_target="tpu_custom_call" | custom-call | tf_op jit(solution)/shard_map/pallas_call | solution.py:488
  27.4 0.8 %copy.4 = bf16[1,27,64,64]{3,2,1,0:T(8,128)(2,1)} copy(bf16[1,27,64,64]{3,2,1,0:T(8,128)(2,1)S(1)} %shard_map.28) | data formatting | bytes 442368
